TPU v7x, 32 devices: a whole 2x2x4 slice. The times are simulated.
32 devices in a mesh: seq: 8 (over z, y), dp: 4 (over x, core).
Axes of the slice: x: 2, y: 2, z: 4, core: 2. Of those that a mesh axis runs over, the one named last changes fastest.
Arguments:
- inputs: bfloat16 [4, 2048, 512], P('dp', 'seq'), may hold values from -6 to 6
- write_vecs: bfloat16 [4, 2048, 128], P('dp', 'seq'), may hold values from -6 to 6
- read_vecs: bfloat16 [4, 2048, 128], P('dp', 'seq'), may hold values from -0.5 to 0.5
- dt_code: int32 [4, 8, 2048], P('dp', None, 'seq'), may hold values from 1 to 10240
- a_rate: float32 [8], replicated, may hold values from 0.4 to 85.333333
- w_out: bfloat16 [512, 2560], replicated, may hold values from -0.125 to 0.125
- grad_out: bfloat16 [4, 2048, 2560], P('dp', 'seq'), may hold values from -0.59765625 to 0.59765625
Outputs:
- outputs: bfloat16 [4, 2048, 512], P('dp', 'seq')
- grad_inputs: bfloat16 [4, 2048, 512], P('dp', 'seq')
- grad_write: bfloat16 [4, 2048, 128], P('dp', 'seq')
- grad_read: bfloat16 [4, 2048, 128], P('dp', 'seq')
- grad_w_out: float32 [512, 2560], P('seq')
All inputs are finite; a program needn't handle non-finite values.
Results may differ from a plain program's by a relative error of at most 0.0055.
Values sent between devices are 32-bit elements; how exact they have to be, the bound alone decides.
A program may use at most 128 MiB of HBM per device.

v0:
```python
import jax
import jax.numpy as jnp
from jax import lax
from jax.sharding import PartitionSpec as P

HEAD_DIM = 64
STATE = 128
LOCAL_HEADS = 8
GROUP = 128


highest = lax.Precision.HIGHEST


def entering(part, axis, combine, identity, reverse):
    count = lax.axis_size(axis)
    place = lax.axis_index(axis)
    ahead = count - 1 - place if reverse else place
    gathered = jax.tree.map(lambda a: lax.all_gather(a, axis), part)
    state = jax.tree.map(lambda a, e: jnp.zeros_like(a) + jnp.asarray(e, a.dtype), part, identity)

    def one(step, state):
        source = count - 1 - step if reverse else step
        return combine(
            state, jax.tree.map(lambda a: lax.dynamic_index_in_dim(a, source, 0, False), gathered)
        )

    return lax.fori_loop(0, ahead, one, state)


def combine(first_part, second_part):
    return (
        first_part[0] * second_part[0],
        second_part[0][:, None, None] * first_part[1] + second_part[1],
    )


def shards(inputs, write_vecs, read_vecs, dt_code, a_rate, w_out, grad_out):
    tokens = inputs.shape[1]
    seq_len = tokens * lax.axis_size("seq")
    blocks = tokens // GROUP
    decay_rate = a_rate / (8.0 * seq_len)
    log_decay = -(decay_rate[:, None] * dt_code[0].astype(jnp.float32))
    weight = jnp.sqrt(-jnp.expm1(2.0 * log_decay))
    weight_rows = weight.reshape(LOCAL_HEADS, blocks, GROUP).transpose(1, 2, 0)[..., None]
    cum_decay = jnp.cumsum(log_decay.reshape(LOCAL_HEADS, blocks, GROUP), axis=2)
    group_last = cum_decay[:, :, -1]
    group_edges = jnp.cumsum(group_last, axis=1)
    totals = jnp.exp(group_edges[:, -1])
    before = jnp.concatenate(
        [jnp.zeros((LOCAL_HEADS, 1), jnp.float32), group_edges[:, :-1]], axis=1
    )
    end_decay = jnp.exp(group_edges[:, -1:] - group_edges)
    start_decay = jnp.exp(before)
    weighted = (
        inputs[0].astype(jnp.float32).reshape(blocks, GROUP, LOCAL_HEADS, HEAD_DIM) * weight_rows
    )
    b_half = write_vecs[0].reshape(blocks, GROUP, STATE)
    c_half = read_vecs[0].reshape(blocks, GROUP, STATE)
    b_rows = b_half.astype(jnp.float32)
    c_rows = c_half.astype(jnp.float32)
    rows_at = lax.broadcasted_iota(jnp.int32, (GROUP, GROUP), 0)
    cols_at = lax.broadcasted_iota(jnp.int32, (GROUP, GROUP), 1)
    spread = cum_decay[:, :, :, None] - cum_decay[:, :, None, :]
    decay_mask = jnp.exp(jnp.where((rows_at >= cols_at)[None, None], spread, -jnp.inf))
    scores = jnp.einsum("kin,kjn->kij", c_half, b_half, preferred_element_type=jnp.float32)
    mixed = decay_mask * scores[None]
    tail_decay = jnp.exp(group_last[:, :, None] - cum_decay)
    tail_rows = tail_decay.transpose(1, 2, 0)[..., None]
    head_decay = jnp.exp(cum_decay).transpose(1, 2, 0)[..., None]
    tailed = weighted * tail_rows
    group_states = jnp.einsum("kjhp,kjn->khpn", tailed, b_rows, precision=highest)
    block_row = lax.broadcasted_iota(jnp.int32, (blocks, blocks), 0)
    block_col = lax.broadcasted_iota(jnp.int32, (blocks, blocks), 1)
    fwd_weights = jnp.exp(
        jnp.where(
            (block_col < block_row)[None], before[:, :, None] - group_edges[:, None, :], -jnp.inf
        )
    )
    bwd_weights = jnp.exp(
        jnp.where(
            (block_col > block_row)[None], before[:, None, :] - group_edges[:, :, None], -jnp.inf
        )
    )
    local_in = jnp.einsum("hkm,mhpn->khpn", fwd_weights, group_states, precision=highest)
    own_state = jnp.einsum("hm,mhpn->hpn", end_decay, group_states, precision=highest)
    grad_rows = grad_out[0]
    grad_y = lax.dot_general(
        grad_rows, w_out, (((1,), (1,)), ((), ())), preferred_element_type=jnp.float32
    ).astype(jnp.bfloat16)
    grad_heads = grad_y.astype(jnp.float32).reshape(blocks, GROUP, LOCAL_HEADS, HEAD_DIM)
    grad_decayed = grad_heads * head_decay
    adj_groups = jnp.einsum("kihp,kin->khpn", grad_decayed, c_rows, precision=highest)
    own_adj = jnp.einsum("hm,mhpn->hpn", start_decay, adj_groups, precision=highest)
    identity = (
        jnp.ones((LOCAL_HEADS,), jnp.float32),
        jnp.zeros((LOCAL_HEADS, HEAD_DIM, STATE), jnp.float32),
    )
    carried_in = entering((totals, own_state), "seq", combine, identity, False)[1]
    adj_later = entering((totals, own_adj), "seq", combine, identity, True)[1]
    state_in = local_in + start_decay.T[:, :, None, None] * carried_in[None]
    y_intra = jnp.einsum("hkij,kjhp->kihp", mixed, weighted, precision=highest)
    y_inter = jnp.einsum("kin,khpn->kihp", c_rows, state_in, precision=highest) * head_decay
    outputs = (y_intra + y_inter).reshape(1, tokens, LOCAL_HEADS * HEAD_DIM).astype(jnp.bfloat16)
    adj_in = (
        jnp.einsum("hkm,mhpn->khpn", bwd_weights, adj_groups, precision=highest)
        + end_decay.T[:, :, None, None] * adj_later[None]
    )
    grad_weighted = jnp.einsum("hkij,kihp->kjhp", mixed, grad_heads, precision=highest)
    grad_weighted = grad_weighted + tail_rows * jnp.einsum(
        "khpn,kjn->kjhp", adj_in, b_rows, precision=highest
    )
    grad_inputs = (
        (grad_weighted * weight_rows)
        .reshape(1, tokens, LOCAL_HEADS * HEAD_DIM)
        .astype(jnp.bfloat16)
    )
    pair_dots = decay_mask * jnp.einsum("kihp,kjhp->hkij", grad_heads, weighted, precision=highest)
    grad_read = jnp.einsum("hkij,kjn->kin", pair_dots, b_rows, precision=highest)
    grad_read = grad_read + jnp.einsum("kihp,khpn->kin", grad_decayed, state_in, precision=highest)
    grad_write = jnp.einsum("hkij,kin->kjn", pair_dots, c_rows, precision=highest)
    grad_write = grad_write + jnp.einsum("kjhp,khpn->kjn", tailed, adj_in, precision=highest)
    grad_read = grad_read.reshape(1, tokens, STATE).astype(jnp.bfloat16)
    grad_write = grad_write.reshape(1, tokens, STATE).astype(jnp.bfloat16)
    out_rows = outputs[0]
    share = lax.psum_scatter(
        lax.dot_general(
            out_rows, grad_rows, (((0,), (0,)), ((), ())), preferred_element_type=jnp.float32
        ),
        "seq",
        scatter_dimension=0,
        tiled=True,
    )
    grad_w_out = lax.psum(share, "dp")
    return (outputs, grad_inputs, grad_write, grad_read, grad_w_out)


def solution(mesh):
    placed = (
        P("dp", "seq", None),
        P("dp", "seq", None),
        P("dp", "seq", None),
        P("dp", None, "seq"),
        P(),
        P(),
        P("dp", "seq", None),
    )
    return jax.shard_map(
        shards,
        mesh=mesh,
        in_specs=placed,
        out_specs=(
            P("dp", "seq", None),
            P("dp", "seq", None),
            P("dp", "seq", None),
            P("dp", "seq", None),
            P("seq", None),
        ),
        check_vma=False,
    )
```

profile of v0, /device:TPU:13, one launch (start us, length us, event | category | flops | bytes accessed | tf_op | source)
XLA Modules:
  0.0 267.6 jit_solution(3431597274971777209)
XLA Ops:
  10.4 2.2 reshape.165
  12.6 1.5 copy.90
  15.3 2.7 %fusion.29 = f32[8,1,64,128]{3,1,2,0:T(1,128)} fusion(f32[8,2,1,1]{1,2,3,0:T(1,128)S(1)} %copy.116, f32[2,8,64,128]{3,2,1,0:T(8,128)S(1)} %fusion.23), kind=kOutput, calls=%fused_computation.44 | convolution fusion | flops 1572864 | bytes 786496 | tf_op jit(solution)/shard_map/hm,mhpn->hpn/dot_general | solution.py:86
  19.4 2.2 fusion.11
  24.7 3.4 %fusion.25 = f32[8,1,64,128]{3,1,2,0:T(1,128)} fusion(f32[8,2,1,1]{1,2,3,0:T(1,128)} %copy.120, f32[2,8,64,128]{3,2,1,0:T(8,128)S(1)} %fusion.21), kind=kOutput, calls=%fused_computation.40 | convolution fusion | flops 1572864 | bytes 786496 | tf_op jit(solution)/shard_map/hm,mhpn->hpn/dot_general | solution.py:94
  28.2 1.3 copy.95
  29.5 1.3 copy.168
  30.8 1.3 copy.91
  35.7 12.2 %all-reduce.1 = f32[64]{0:T(128)} all-reduce(f32[64]{0:T(128)} %bitcast_dynamic-update-slice_fusion), channel_id=2, replica_groups=mesh['seq'=8,'dp'=4] {'seq'}, use_global_device_ids=true, to_apply=%add.1 | all-reduce | flops 64 | bytes 512
  47.9 1.3 reshape.146
  51.5 4.0 %fusion.31 = f32[8,64,128,2]{2,3,1,0:T(2,128)} fusion(f32[2,8,64,128]{3,2,1,0:T(8,128)} %copy-done.6, pred[2,2]{1,0:T(4,128)(4,1)S(1)} %iota_compare_fusion.2, f32[8,2]{1,0:T(8,128)} %copy.95, f32[8,2]{1,0:T(8,128)S(1)} %concatenate.3.clone), kind=kOutput, calls=%fused_computation.46 | convolution fusion | flops 3145792 | bytes 1048708 | tf_op jit(solution)/shard_map/hkm,mhpn->khpn/dot_general | solution.py:85
  55.5 11.6 %all-gather.6.cloned.1.call-done = f32[64,64,128]{2,1,0:T(8,128)} async-done(((f32[8,64,128]{2,1,0:T(8,128)}), f32[64,64,128]{2,1,0:T(8,128)}) %all-gather.6.cloned.1.call-update) | async-done | bytes 2097168 | tf_op jit(solution)/shard_map/all_gather | solution.py:19
  67.1 5.5 %while.26 = (s32[]{:T(128)}, f32[8,64,128]{2,1,0:T(8,128)S(1)}, s32[]{:T(128)}, f32[8,8]{1,0:T(8,128)}, f32[8,8,64,128]{3,2,1,0:T(8,128)}, /*index=5*/s32[]{:T(128)}, s32[]{:T(128)}, s32[]{:T(128)}) while((s32[]{:T(128)}, f32[8,64,128]{2,1,0:T(8,128)S(1)}, s32[]{:T(128)}, f32[8,8]{1,0:T(8,128)}, f32[8,8,64,128]{3,2,1,0:T(8,128)}, ...), condition=%wide.region_3.4_spmd, body=%wide.region_2.3_spmd.sunk | while | flops 131077 | bytes 786663 | solution.py:28
  72.6 1.6 fusion.8
  74.2 3.1 %fusion.10 = bf16[2,128,8,64]{1,3,2,0:T(8,128)(2,1)S(1)} fusion(f32[2,128,8,64]{1,3,2,0:T(8,128)S(1)} %fusion.8, f32[2,128,128]{2,1,0:T(8,128)} %fusion.74, f32[8,2,128]{2,1,0:T(2,128)} %copy.91, pred[128,128]{1,0:T(8,128)(4,1)} %iota_compare_fusion, f32[2,128,8,64]{1,3,2,0:T(8,128)S(1)} %copy.90, f32[2,128,8]{1,2,0:T(8,128)} %copy-done.13), kind=kOutput, calls=%fused_computation.19 | convolution fusion | flops 202506240 | bytes 1474560 | tf_op jit(solution)/shard_map/hkij,kjhp->kihp/dot_general | solution.py:102
  78.3 3.1 %fusion = f32[512,2560]{1,0:T(8,128)} fusion(bf16[1,256,2560]{2,1,0:T(8,128)(2,1)S(1)} %copy-done.7, bf16[64,8,2,128]{3,2,1,0:T(2,128)(2,1)S(1)} %bitcast.148), kind=kOutput, calls=%fused_computation.5 | convolution fusion | flops 671088640 | bytes 6815744 | tf_op jit(solution)/shard_map/dot_general | solution.py:127
  81.6 2.6 fusion.4
  84.1 2.9 %fusion.27 = f32[8,64,128,2]{2,3,1,0:T(2,128)} fusion(f32[2,8,64,128]{3,2,1,0:T(8,128)S(1)} %copy-done.5, pred[2,2]{1,0:T(4,128)(4,1)S(1)} %iota_compare_fusion.1, f32[8,2]{1,0:T(8,128)S(1)} %copy-done.14, f32[8,2]{1,0:T(8,128)S(1)} %copy-done.16), kind=kOutput, calls=%fused_computation.42 | convolution fusion | flops 3145792 | bytes 1048708 | tf_op jit(solution)/shard_map/hkm,mhpn->khpn/dot_general | solution.py:106
  87.0 2.0 copy.127
  89.0 28.8 %all-gather.8.cloned.1.call-done = f32[64,64,128]{2,1,0:T(8,128)} async-done(((f32[8,64,128]{2,1,0:T(8,128)}), f32[64,64,128]{2,1,0:T(8,128)}) %all-gather.8.cloned.1.call-update) | async-done | bytes 2097168 | tf_op jit(solution)/shard_map/all_gather | solution.py:19
  117.8 7.1 %while.27 = (s32[]{:T(128)}, f32[8,64,128]{2,1,0:T(8,128)S(1)}, s32[]{:T(128)}, f32[8,8]{1,0:T(8,128)}, f32[8,8,64,128]{3,2,1,0:T(8,128)}, /*index=5*/s32[]{:T(128)}, s32[]{:T(128)}, s32[]{:T(128)}, s32[]{:T(128)}) while((s32[]{:T(128)}, f32[8,64,128]{2,1,0:T(8,128)S(1)}, s32[]{:T(128)}, f32[8,8]{1,0:T(8,128)}, f32[8,8,64,128]{3,2,1,0:T(8,128)}, ...), condition=%wide.region_5.6_spmd, body=%wide.region_4.5_spmd.sunk | while | flops 131078 | bytes 786683 | solution.py:28
  125.0 1.5 fusion.9
  126.5 2.5 fusion.14
  129.0 2.1 copy.128
  131.1 2.1 reshape.167
  133.2 2.1 reshape.166
  135.3 2.3 convolution_bitcast_fusion.5
  137.6 1.9 fusion.15
  139.5 84.6 %reduce-scatter.2.cloned.1.call-done = f32[64,2560]{1,0:T(8,128)} async-done(((f32[512,2560]{1,0:T(8,128)}), f32[64,2560]{1,0:T(8,128)}) %reduce-scatter.2.cloned.1.call-update) | async-done | bytes 655376 | tf_op jit(solution)/shard_map/reduce_scatter | solution.py:126
  224.1 2.1 convolution_bitcast_fusion.4
  227.1 32.0 %all-reduce.4.cloned.1.call-done = f32[64,2560]{1,0:T(8,128)} async-done(((f32[64,2560]{1,0:T(8,128)}), f32[64,2560]{1,0:T(8,128)}) %all-reduce.4.cloned.1.call-update) | async-done | bytes 655376 | tf_op jit(solution)/shard_map/psum | solution.py:134
  259.1 2.0 copy.186
  (87 shorter events, 28.2 us)
Async XLA Ops:
  7.2 12.2 %copy-start = (bf16[512,2560]{1,0:T(8,128)(2,1)S(1)}, bf16[512,2560]{1,0:T(8,128)(2,1)}, u32[]{:S(2)}) copy-start(bf16[512,2560]{1,0:T(8,128)(2,1)} %param.16) | copy-start | bytes 7864324
  7.2 6.9 %copy-start.9 = (bf16[1,256,128]{2,1,0:T(8,128)(2,1)S(1)}, bf16[1,256,128]{2,1,0:T(8,128)(2,1)}, u32[]{:S(2)}) copy-start(bf16[1,256,128]{2,1,0:T(8,128)(2,1)} %param.12) | copy-start | bytes 196612
  7.2 59.9 %all-gather.6.cloned.1.call-start = ((), (), s32[]{:S(2)}) async-start(), calls=%async_computation.3 | async-start | bytes 2359296 | tf_op jit(solution)/shard_map/all_gather | solution.py:19
  8.8 9.2 %copy-start.13 = (f32[2,128,8]{1,2,0:T(8,128)}, f32[2,128,8]{1,2,0:T(8,128)S(1)}, u32[]{:S(2)}) copy-start(f32[2,128,8]{1,2,0:T(8,128)S(1)} %get-tuple-element.170) | copy-start | bytes 24580
  9.4 8.6 %copy-start.12 = (f32[8,2,128]{2,0,1:T(8,128)}, f32[8,2,128]{2,0,1:T(8,128)S(1)}, u32[]{:S(2)}) copy-start(f32[8,2,128]{2,0,1:T(8,128)S(1)} %reduce_window_sum.24) | copy-start | bytes 24580
  9.6 0.8 copy-start.17
  9.6 8.5 %copy-start.18 = (f32[8,1]{0,1:T(1,128)}, f32[8,1]{0,1:T(1,128)S(1)}, u32[]{:S(2)}) copy-start(f32[8,1]{0,1:T(1,128)S(1)} %get-tuple-element.177) | copy-start | bytes 100
  14.1 67.5 %copy-start.1 = (f32[2,128,8,64]{1,3,2,0:T(8,128)}, f32[2,128,8,64]{1,3,2,0:T(8,128)S(1)}, u32[]{:S(2)}) copy-start(f32[2,128,8,64]{1,3,2,0:T(8,128)S(1)} %copy.90) | copy-start | bytes 1572868
  14.5 0.8 copy-start.6
  18.1 99.7 %all-gather.8.cloned.1.call-start = ((), (), s32[]{:S(2)}) async-start(), calls=%async_computation.4 | async-start | bytes 2359296 | tf_op jit(solution)/shard_map/all_gather | solution.py:19
  19.4 4.1 %copy-start.10 = (bf16[1,256,128]{2,1,0:T(8,128)(2,1)S(1)}, bf16[1,256,128]{2,1,0:T(8,128)(2,1)}, u32[]{:S(2)}) copy-start(bf16[1,256,128]{2,1,0:T(8,128)(2,1)} %param.13) | copy-start | bytes 196612
  23.5 43.6 %copy-start.2 = (bf16[2,128,8,64]{1,0,3,2:T(2,128)(2,1)}, bf16[2,128,8,64]{1,0,3,2:T(2,128)(2,1)S(1)}, u32[]{:S(2)}) copy-start(bf16[2,128,8,64]{1,0,3,2:T(2,128)(2,1)S(1)} %reshape.143) | copy-start | bytes 786436
  23.9 0.8 copy-start.4
  28.2 195.9 %reduce-scatter.2.cloned.1.call-start = ((), (), s32[]{:S(2)}) async-start(), calls=%async_computation.1 | async-start | bytes 5898240 | tf_op jit(solution)/shard_map/reduce_scatter | solution.py:126
  50.0 1.5 copy-start.15
  72.6 5.7 %copy-start.7 = (bf16[1,256,2560]{2,1,0:T(8,128)(2,1)S(1)}, bf16[1,256,2560]{2,1,0:T(8,128)(2,1)}, u32[]{:S(2)}) copy-start(bf16[1,256,2560]{2,1,0:T(8,128)(2,1)} %param.17) | copy-start | bytes 3932164
  77.3 0.7 copy-start.8
  81.5 177.6 %all-reduce.4.cloned.1.call-start = ((), (), s32[]{:S(2)}) async-start(), calls=%async_computation.2 | async-start | bytes 1310720 | tf_op jit(solution)/shard_map/psum | solution.py:134
  81.5 2.6 copy-start.5
  81.5 2.6 copy-start.14
  81.5 2.6 copy-start.16
  117.8 8.6 %copy-start.3 = (bf16[2,128,8,64]{1,0,3,2:T(2,128)(2,1)S(1)}, bf16[2,128,8,64]{1,0,3,2:T(2,128)(2,1)}, u32[]{:S(2)}) copy-start(bf16[2,128,8,64]{1,0,3,2:T(2,128)(2,1)} %copy-done.2) | copy-start | bytes 786436
  137.6 88.7 %copy-start.11 = (f32[2,128,128]{2,1,0:T(8,128)S(1)}, f32[2,128,128]{2,1,0:T(8,128)}, u32[]{:S(2)}) copy-start(f32[2,128,128]{2,1,0:T(8,128)} %fusion.4) | copy-start | bytes 393220
Sparse Core Ops, SparseCore 0:
  18.2 48.8 all-gather.5
  69.8 47.9 all-gather.7
  121.4 102.6 reduce-scatter.1
  226.3 32.7 all-reduce.3
where the time goes:
time: 271 us; the launch traced here: 268 us
  waiting for transfers between devices  157 us (58%)
  matrix products  38.4 us (14%)
  local copies, waits for them, and re-layouts  33.8 us (12%)
  between operations  14.7 us (5%)
  blocking collectives  12.2 us (5%)
  other arithmetic  10.9 us (4%)
    reduce_scatter x1, waiting for transfers between devices, shards(): lax.psum_scatter(lax.dot_general(out_rows, grad_rows, (((0,), (0,)), ((),...  84.6 us
    all_gather x2, waiting for transfers between devices, entering(): gathered = jax.tree.map(lambda a: lax.all_gather(a, axis), part)  40.4 us
    psum x1, waiting for transfers between devices, shards(): grad_w_out = lax.psum(share, 'dp')  32 us
    unnamed x47, local copies, waits for them, and re-layouts  16.9 us
    unnamed x1, blocking collectives  12.2 us
    add x7, other arithmetic, combine(): second_part[0][:, None, None] * first_part[1] + second_part[1]  7.38 us
  transfers between devices with their start and end apart: 4, of which 4 were waited for; matrix products, arithmetic and copies ran while one was open for 26% of the time, Pallas kernels for 0%

commit v1 on v0

v1 whole, which is shorter than its diff:
```python
import functools

import jax
import jax.numpy as jnp
from jax import lax
from jax.experimental import pallas as pl
from jax.experimental.pallas import tpu as pltpu
from jax.sharding import PartitionSpec as P

HEAD_DIM = 64
STATE = 128
HEADS = 8
CHANNELS = HEADS * HEAD_DIM
MESH = pl.DeviceIdType.MESH
f32 = jnp.float32
bf16 = jnp.bfloat16


def dot(a, b, dims=((1,), (0,))):
    return lax.dot_general(a, b, (dims, ((), ())), preferred_element_type=f32)


NT = ((1,), (1,))
TN = ((0,), (0,))


def widen(cols):
    rows = cols.shape[0]
    return jnp.concatenate(
        [jnp.broadcast_to(cols[:, h : h + 1], (rows, HEAD_DIM)) for h in range(HEADS)], axis=1
    )


def one_minus_exp(w):
    series = 1.0 - w * (1.0 / 9.0)
    for k in (8, 7, 6, 5, 4, 3, 2):
        series = 1.0 - w * (1.0 / k) * series
    return jnp.where(w < 0.5, w * series, 1.0 - jnp.exp(-w))


def kernel(
    n, m, seq_len,
    x_ref, b_ref, c_ref, dt_ref, arow_ref, acol_ref, w_ref, g_ref,
    out_ref, gin_ref, gwrite_ref, gread_ref, gw_ref,
    gsend, gall, fsend, frecv, fback, fin, asend, arecv, aback, ain,
    oall, part, rsbuf, gwall,
    g_ss, g_rs, f_ss, f_rs, a_ss, a_rs, fb_ss, fb_rs, ab_ss, ab_rs,
    o_ss, o_rs, r_ss, r_rs, w_ss, w_rs,
):
    me = lax.axis_index("seq")
    dp = lax.axis_index("dp")
    tokens = x_ref.shape[1]
    rows = CHANNELS // n
    per_head = HEAD_DIM // rows
    cols = gsend.shape[2]

    def seq_copy(src, dst, ss, rs, k, wait):
        to = lax.rem(me + k, n)
        source = lax.rem(me + n - k, n)
        return pltpu.make_async_remote_copy(
            src_ref=src.at[to],
            dst_ref=dst.at[source] if wait else dst.at[me],
            send_sem=ss.at[k],
            recv_sem=rs.at[k],
            device_id={"seq": to},
            device_id_type=MESH,
        )

    def seq_start(src, dst, ss, rs):
        def body(k, carry):
            seq_copy(src, dst, ss, rs, k, False).start()
            return carry

        lax.fori_loop(1, n, body, 0)

    def seq_wait(src, dst, ss, rs):
        def body(k, carry):
            seq_copy(src, dst, ss, rs, k, True).wait()
            return carry

        lax.fori_loop(1, n, body, 0)

    def dp_copy(src, dst, ss, rs, k, wait):
        to = lax.rem(dp + k, m)
        source = lax.rem(dp + m - k, m)
        return pltpu.make_async_remote_copy(
            src_ref=src.at[to],
            dst_ref=dst.at[source] if wait else dst.at[dp],
            send_sem=ss.at[k],
            recv_sem=rs.at[k],
            device_id={"dp": to},
            device_id_type=MESH,
        )

    def dp_gather(buf, ss, rs):
        held, bit, copies = [0], m // 2, []
        while bit:
            step = []
            for off in held:
                slot = jnp.bitwise_xor(dp, off)
                copy = pltpu.make_async_remote_copy(
                    src_ref=buf.at[slot],
                    dst_ref=buf.at[slot],
                    send_sem=ss.at[off + bit],
                    recv_sem=rs.at[off + bit],
                    device_id={"dp": jnp.bitwise_xor(dp, bit)},
                    device_id_type=MESH,
                )
                copy.start()
                step.append(copy)
            for off in held:
                slot = jnp.bitwise_xor(dp, off + bit)
                pltpu.make_async_remote_copy(
                    src_ref=buf.at[slot],
                    dst_ref=buf.at[slot],
                    send_sem=ss.at[off + bit],
                    recv_sem=rs.at[off + bit],
                    device_id={"dp": jnp.bitwise_xor(dp, bit)},
                    device_id_type=MESH,
                ).wait_recv()
            copies += step
            held = held + [off + bit for off in held]
            bit //= 2
        for copy in copies:
            copy.wait_send()

    barrier = pltpu.get_barrier_semaphore()

    def greet_seq(k, carry):
        pl.semaphore_signal(
            barrier, inc=1, device_id={"seq": lax.rem(me + k, n)}, device_id_type=MESH
        )
        return carry

    def greet_dp(k, carry):
        pl.semaphore_signal(
            barrier, inc=1, device_id={"dp": lax.rem(dp + k, m)}, device_id_type=MESH
        )
        return carry

    lax.fori_loop(1, n, greet_seq, 0)
    lax.fori_loop(1, m, greet_dp, 0)

    dt = dt_ref[0]
    at_row = lax.broadcasted_iota(jnp.int32, (tokens, tokens), 0)
    at_col = lax.broadcasted_iota(jnp.int32, (tokens, tokens), 1)
    lower = at_row >= at_col
    low_mat = lower.astype(f32).astype(bf16)
    eye = (at_row == at_col).astype(f32).astype(bf16)
    digits = [
        part_of.astype(f32).astype(bf16) for part_of in (dt & 127, (dt >> 7) & 127, dt >> 14)
    ]

    def joined(pieces):
        whole = [p.astype(jnp.int32) for p in pieces]
        return whole[0] + whole[1] * 128 + whole[2] * 16384

    cum_row = joined([dot(d, low_mat, NT) for d in digits])
    cum_col = joined([dot(low_mat, d, NT) for d in digits])
    dt_col = joined([dot(eye, d, NT) for d in digits])
    rate_row = arow_ref[...] * (1.0 / (8.0 * seq_len))
    rate_col = acol_ref[...] * (1.0 / (8.0 * seq_len))
    weight = jnp.sqrt(one_minus_exp(2.0 * (rate_row * dt_col.astype(f32))))
    head = jnp.exp(-(rate_row * cum_col.astype(f32)))
    tail = jnp.exp(-(rate_row * (cum_col[tokens - 1 :, :] - cum_col).astype(f32)))
    totals = jnp.broadcast_to(
        jnp.exp(-(rate_col * cum_row[:, tokens - 1 :].astype(f32))), (HEADS, STATE)
    )
    weight_w, head_w, tail_w = widen(weight), widen(head), widen(tail)

    b = b_ref[0]
    c = c_ref[0]
    weighted = x_ref[0].astype(f32) * weight_w
    tailed = (weighted * tail_w).astype(bf16)
    weighted = weighted.astype(bf16)
    own = dot(tailed, b, TN)
    fsend[:, :rows, :] = own.reshape(n, rows, STATE)
    fsend[:, rows:, :] = jnp.broadcast_to(totals[None], (n, HEADS, STATE))

    pl.semaphore_wait(barrier, n - 1 + m - 1)
    seq_start(fsend, frecv, f_ss, f_rs)

    grad = g_ref[0]
    for d in range(m):
        gsend[d] = grad[:, d * cols : (d + 1) * cols].astype(f32)

    def g_start(k, carry):
        dp_copy(gsend, gall, g_ss, g_rs, k, False).start()
        return carry

    def g_wait(k, carry):
        dp_copy(gsend, gall, g_ss, g_rs, k, True).wait()
        return carry

    lax.fori_loop(1, m, g_start, 0)
    gall[dp] = gsend[dp]

    grad_y = dot(grad, w_ref[...], NT).astype(bf16)
    grad_dec = (grad_y.astype(f32) * head_w).astype(bf16)
    own_adj = dot(grad_dec, c, TN)
    asend[:, :rows, :] = own_adj.reshape(n, rows, STATE)
    asend[:, rows:, :] = jnp.broadcast_to(totals[None], (n, HEADS, STATE))
    seq_start(asend, arecv, a_ss, a_rs)

    my_head = (me * rows) // HEAD_DIM
    frecv[me] = fsend[me]
    arecv[me] = asend[me]

    def scan_rows(buf, back, reverse):
        def body(step, state):
            s = n - 1 - step if reverse else step
            back[s] = state
            decay = buf[s, pl.ds(rows + my_head, 1), :]
            return decay * state + buf[s, :rows, :]

        lax.fori_loop(0, n, body, jnp.zeros((rows, STATE), f32))

    seq_wait(fsend, frecv, f_ss, f_rs)
    scan_rows(frecv, fback, False)
    seq_start(fback, fin, fb_ss, fb_rs)
    fin[me] = fback[me]
    seq_wait(asend, arecv, a_ss, a_rs)
    scan_rows(arecv, aback, True)
    seq_start(aback, ain, ab_ss, ab_rs)
    ain[me] = aback[me]

    scores = dot(c, b, NT)
    pair = jnp.zeros((tokens, tokens), f32)
    y_parts, gx_parts = [], []
    for h in range(HEADS):
        span = slice(h * HEAD_DIM, (h + 1) * HEAD_DIM)
        gap = (cum_col[:, h : h + 1] - cum_row[h : h + 1, :]).astype(f32)
        mask = jnp.exp(jnp.where(lower, -(rate_row[:, h : h + 1] * gap), -jnp.inf))
        mixed = (mask * scores).astype(bf16)
        w_h, g_h = weighted[:, span], grad_y[:, span]
        y_parts.append(dot(mixed, w_h))
        gx_parts.append(dot(mixed, g_h, TN))
        pair = pair + mask * dot(g_h, w_h, NT)
    y_intra = jnp.concatenate(y_parts, axis=1)
    gx_intra = jnp.concatenate(gx_parts, axis=1)
    pair = pair.astype(bf16)
    read_intra = dot(pair, b)
    write_intra = dot(pair, c, TN)

    seq_wait(fback, fin, fb_ss, fb_rs)
    state_in = fin[...].reshape(CHANNELS, STATE).astype(bf16)
    out = (y_intra + dot(c, state_in, NT) * head_w).astype(bf16)
    out_ref[0] = out
    oall[dp] = out.astype(f32)
    dp_gather(oall, o_ss, o_rs)
    lax.fori_loop(1, m, g_wait, 0)
    total = jnp.zeros((CHANNELS, cols), f32)
    for d in range(m):
        total = total + dot(oall[d].astype(bf16), gall[d].astype(bf16), TN)
    part[...] = total.reshape(n, rows, cols)
    seq_start(part, rsbuf, r_ss, r_rs)

    gread_ref[0] = (read_intra + dot(grad_dec, state_in)).astype(bf16)
    seq_wait(aback, ain, ab_ss, ab_rs)
    adj_in = ain[...].reshape(CHANNELS, STATE).astype(bf16)
    gwrite_ref[0] = (write_intra + dot(tailed, adj_in)).astype(bf16)
    gin_ref[0] = ((gx_intra + tail_w * dot(b, adj_in, NT)) * weight_w).astype(bf16)

    def add_rows(k, acc):
        seq_copy(part, rsbuf, r_ss, r_rs, k, True).wait()
        return acc + rsbuf[lax.rem(me + n - k, n)]

    gwall[dp] = lax.fori_loop(1, n, add_rows, part[me])
    dp_gather(gwall, w_ss, w_rs)
    for d in range(m):
        gw_ref[:, d * cols : (d + 1) * cols] = gwall[d]


def solution(mesh):
    n, m = mesh.shape["seq"], mesh.shape["dp"]

    def shards(inputs, write_vecs, read_vecs, dt_code, a_rate, w_out, grad_out):
        tokens, width = inputs.shape[1], grad_out.shape[2]
        rows, cols = CHANNELS // n, width // m
        vm = pl.BlockSpec(memory_space=pltpu.VMEM)
        sems = []
        for count in (m, n, n, n, n, m, n, m):
            sems += [pltpu.SemaphoreType.DMA((count,))] * 2
        wide, plain = (n, rows + HEADS, STATE), (n, rows, STATE)
        return pl.pallas_call(
            functools.partial(kernel, n, m, float(tokens * n)),
            out_shape=(
                jax.ShapeDtypeStruct((1, tokens, CHANNELS), bf16),
                jax.ShapeDtypeStruct((1, tokens, CHANNELS), bf16),
                jax.ShapeDtypeStruct((1, tokens, STATE), bf16),
                jax.ShapeDtypeStruct((1, tokens, STATE), bf16),
                jax.ShapeDtypeStruct((rows, width), f32),
            ),
            in_specs=[vm] * 8,
            out_specs=(vm,) * 5,
            scratch_shapes=[
                pltpu.VMEM((m, tokens, cols), f32),
                pltpu.VMEM((m, tokens, cols), f32),
                pltpu.VMEM(wide, f32),
                pltpu.VMEM(wide, f32),
                pltpu.VMEM(plain, f32),
                pltpu.VMEM(plain, f32),
                pltpu.VMEM(wide, f32),
                pltpu.VMEM(wide, f32),
                pltpu.VMEM(plain, f32),
                pltpu.VMEM(plain, f32),
                pltpu.VMEM((m, tokens, CHANNELS), f32),
                pltpu.VMEM((n, rows, cols), f32),
                pltpu.VMEM((n, rows, cols), f32),
                pltpu.VMEM((m, rows, cols), f32),
            ]
            + sems,
            compiler_params=pltpu.CompilerParams(
                collective_id=0, has_side_effects=True, vmem_limit_bytes=48 * 1024 * 1024
            ),
            name="scan_core",
        )(
            inputs,
            write_vecs,
            read_vecs,
            dt_code,
            a_rate.reshape(1, HEADS),
            a_rate.reshape(HEADS, 1),
            w_out,
            grad_out,
        )

    placed = (
        P("dp", "seq", None),
        P("dp", "seq", None),
        P("dp", "seq", None),
        P("dp", None, "seq"),
        P(),
        P(),
        P("dp", "seq", None),
    )
    return jax.shard_map(
        shards,
        mesh=mesh,
        in_specs=placed,
        out_specs=(
            P("dp", "seq", None),
            P("dp", "seq", None),
            P("dp", "seq", None),
            P("dp", "seq", None),
            P("seq", None),
        ),
        check_vma=False,
    )
```

time: 271 us -> 98.3 us (0.36); the launches traced: 268 us -> 97.9 us
  waiting for transfers between devices: 157 us -> 0 us
  Pallas kernels: 0 us -> 86 us
  matrix products: 38.4 us -> 0 us
  local copies, waits for them, and re-layouts: 33.8 us -> 11.3 us
  between operations: 14.7 us -> 0.65 us
  blocking collectives: 12.2 us -> 0 us
  other arithmetic: 10.9 us -> 0 us
    pallas_call x0 -> x1, Pallas kernels: none -> 86 us  [shards(): pl.pallas_call(functools.partial(kernel, n, m, float(tokens * n)), out_sh...]
    reduce_scatter x1 -> x0, waiting for transfers between devices: 84.6 us -> none  [shards(): lax.psum_scatter(lax.dot_general(out_rows, grad_rows, (((0,), (0,)), ((),...]
    all_gather x2 -> x0, waiting for transfers between devices: 40.4 us -> none  [entering(): gathered = jax.tree.map(lambda a: lax.all_gather(a, axis), part)]
    dot_general x18 -> x0, matrix products: 38.4 us -> none  [the longest x1 3.99 us: shards(): jnp.einsum('hkm,mhpn->khpn', fwd_weights, group_states, precision=highest)]
    psum x1 -> x0, waiting for transfers between devices: 32 us -> none  [shards(): grad_w_out = lax.psum(share, 'dp')]
    unnamed x1 -> x0, blocking collectives: 12.2 us -> none
    add x7 -> x0, other arithmetic: 7.38 us -> none  [combine(): second_part[0][:, None, None] * first_part[1] + second_part[1]]
    unnamed x47 -> x19, local copies, waits for them, and re-layouts: 16.9 us -> 10.5 us
  transfers between devices with their start and end apart: 4 -> 0, of which waited for: 4 -> 0; matrix products, arithmetic and copies ran while one was open for 26% -> 0% of each run, Pallas kernels for 0% -> 0%
where the time goes in v1:
time: 98.3 us; the launch traced here: 97.9 us
  Pallas kernels  86 us (87%)
  local copies, waits for them, and re-layouts  11.3 us (11%)
    pallas_call x1, Pallas kernels, shards(): pl.pallas_call(functools.partial(kernel, n, m, float(tokens * n)), out_sh...  86 us
    unnamed x19, local copies, waits for them, and re-layouts  10.5 us

profile of v1, /device:TPU:13, one launch (start us, length us, event | category | flops | bytes accessed | tf_op | source)
XLA Modules:
  0.0 97.9 jit_solution(13428330446408378426)
XLA Ops:
  0.6 0.7 copy.12.acol_ref
  1.4 0.0 copy-start
  1.4 1.7 %copy-done = bf16[512,2560]{1,0:T(8,128)(2,1)S(1)} copy-done((bf16[512,2560]{1,0:T(8,128)(2,1)S(1)}, bf16[512,2560]{1,0:T(8,128)(2,1)}, u32[]{:S(2)}) %copy-start) | copy-done | bytes 2621464
  3.1 0.0 copy-start.1
  3.1 1.3 %copy-done.1 = bf16[1,256,2560]{2,1,0:T(8,128)(2,1)S(1)} copy-done((bf16[1,256,2560]{2,1,0:T(8,128)(2,1)S(1)}, bf16[1,256,2560]{2,1,0:T(8,128)(2,1)}, u32[]{:S(2)}) %copy-start.1) | copy-done | bytes 1310744
  4.4 0.0 copy-start.2
  4.4 0.9 copy-done.2
  5.4 0.0 copy-start.3
  5.4 0.8 copy-done.3
  6.2 0.0 copy-start.4
  6.2 0.8 copy-done.4
  7.1 0.0 copy-start.5
  7.1 0.7 copy-done.5
  7.7 0.0 copy-start.6
  7.8 0.7 copy-done.6
  8.4 86.0 %scan_core.1 = (bf16[1,256,512]{2,1,0:T(8,128)(2,1)S(1)}, bf16[1,256,512]{2,1,0:T(8,128)(2,1)S(1)}, bf16[1,256,128]{2,1,0:T(8,128)(2,1)S(1)}, bf16[1,256,128]{2,1,0:T(8,128)(2,1)S(1)}, f32[64,2560]{1,0:T(8,128)S(1)}) custom-call(bf16[1,256,512]{2,1,0:T(8,128)(2,1)S(1)} %copy-done.2, bf16[1,256,128]{2,1,0:T(8,128)(2,1)S(1)} %copy-done.3, ...), custom_call_target="tpu_custom_call" | custom-call | tf_op jit(solution)/shard_map/scan_core/pallas_call | solution.py:285
  94.4 0.7 copy.18
  95.1 0.7 copy.19
  95.8 0.6 copy.20
  96.4 0.6 copy.21
  97.1 0.8 copy.22
Async XLA Ops:
  1.4 1.7 %copy-start = (bf16[512,2560]{1,0:T(8,128)(2,1)S(1)}, bf16[512,2560]{1,0:T(8,128)(2,1)}, u32[]{:S(2)}) copy-start(bf16[512,2560]{1,0:T(8,128)(2,1)} %w_ref.1) | copy-start | bytes 7864324
  3.1 1.3 %copy-start.1 = (bf16[1,256,2560]{2,1,0:T(8,128)(2,1)S(1)}, bf16[1,256,2560]{2,1,0:T(8,128)(2,1)}, u32[]{:S(2)}) copy-start(bf16[1,256,2560]{2,1,0:T(8,128)(2,1)} %g_ref.1) | copy-start | bytes 3932164
  4.4 0.9 copy-start.2
  5.4 0.8 copy-start.3
  6.2 0.8 copy-start.4
  7.1 0.7 copy-start.5
  7.7 0.7 copy-start.6

commit v2 on v1

--- a/solution.py
+++ b/solution.py
@@ -10,6 +10,9 @@
 HEAD_DIM = 64
 STATE = 128
 HEADS = 8
+CHUNKS = 4
+ORDER = (0, 3, 1, 2)
+VMEM_BYTES = 60 * 1024 * 1024
 CHANNELS = HEADS * HEAD_DIM
 MESH = pl.DeviceIdType.MESH
 f32 = jnp.float32
@@ -40,16 +43,34 @@
 
 def kernel(
     n, m, seq_len,
-    x_ref, b_ref, c_ref, dt_ref, arow_ref, acol_ref, w_ref, g_ref,
+    x_hbm, b_hbm, c_hbm, dt_hbm, arow_ref, w_hbm, g_hbm,
+    out_hbm, gin_hbm, gwrite_hbm, gread_hbm, gw_hbm,
+    x_ref, b_ref, c_ref, dt_ref, w_ref, g_ref,
     out_ref, gin_ref, gwrite_ref, gread_ref, gw_ref,
     gsend, gall, fsend, frecv, fback, fin, asend, arecv, aback, ain,
-    oall, part, rsbuf, gwall,
+    oall, part, ybuf, rsbuf, gwall,
     g_ss, g_rs, f_ss, f_rs, a_ss, a_rs, fb_ss, fb_rs, ab_ss, ab_rs,
-    o_ss, o_rs, r_ss, r_rs, w_ss, w_rs,
+    o_ss, o_rs, y_ss, y_rs, r_ss, r_rs, w_ss, w_rs, in_sem, out_sem,
 ):
     me = lax.axis_index("seq")
     dp = lax.axis_index("dp")
     tokens = x_ref.shape[1]
+    pairs = n // 2
+    z, y = me // 2, lax.rem(me, 2)
+    loads = [
+        pltpu.make_async_copy(src, dst, in_sem.at[i])
+        for i, (src, dst) in enumerate(
+            [(dt_hbm, dt_ref), (x_hbm, x_ref), (b_hbm, b_ref), (c_hbm, c_ref), (g_hbm, g_ref), (w_hbm, w_ref)]
+        )
+    ]
+    for load in loads:
+        load.start()
+    stores = [
+        pltpu.make_async_copy(src, dst, out_sem.at[i])
+        for i, (src, dst) in enumerate(
+            [(out_ref, out_hbm), (gin_ref, gin_hbm), (gwrite_ref, gwrite_hbm), (gread_ref, gread_hbm), (gw_ref, gw_hbm)]
+        )
+    ]
     rows = CHANNELS // n
     per_head = HEAD_DIM // rows
     cols = gsend.shape[2]
@@ -92,37 +113,51 @@
             device_id_type=MESH,
         )
 
-    def dp_gather(buf, ss, rs):
-        held, bit, copies = [0], m // 2, []
-        while bit:
-            step = []
-            for off in held:
-                slot = jnp.bitwise_xor(dp, off)
-                copy = pltpu.make_async_remote_copy(
-                    src_ref=buf.at[slot],
-                    dst_ref=buf.at[slot],
-                    send_sem=ss.at[off + bit],
-                    recv_sem=rs.at[off + bit],
-                    device_id={"dp": jnp.bitwise_xor(dp, bit)},
-                    device_id_type=MESH,
-                )
-                copy.start()
-                step.append(copy)
-            for off in held:
-                slot = jnp.bitwise_xor(dp, off + bit)
-                pltpu.make_async_remote_copy(
-                    src_ref=buf.at[slot],
-                    dst_ref=buf.at[slot],
-                    send_sem=ss.at[off + bit],
-                    recv_sem=rs.at[off + bit],
-                    device_id={"dp": jnp.bitwise_xor(dp, bit)},
-                    device_id_type=MESH,
-                ).wait_recv()
-            copies += step
-            held = held + [off + bit for off in held]
-            bit //= 2
-        for copy in copies:
-            copy.wait_send()
+    bits = [1 << i for i in reversed(range(m.bit_length() - 1))]
+
+    def dp_send(buf, ss, rs, off, bit):
+        slot = jnp.bitwise_xor(dp, off)
+        return pltpu.make_async_remote_copy(
+            src_ref=buf.at[slot],
+            dst_ref=buf.at[slot],
+            send_sem=ss.at[off + bit],
+            recv_sem=rs.at[off + bit],
+            device_id={"dp": jnp.bitwise_xor(dp, bit)},
+            device_id_type=MESH,
+        )
+
+    def dp_arrived(buf, ss, rs, off):
+        slot = jnp.bitwise_xor(dp, off)
+        bit = off & -off
+        pltpu.make_async_remote_copy(
+            src_ref=buf.at[slot],
+            dst_ref=buf.at[slot],
+            send_sem=ss.at[off],
+            recv_sem=rs.at[off],
+            device_id={"dp": jnp.bitwise_xor(dp, bit)},
+            device_id_type=MESH,
+        ).wait_recv()
+
+    def dp_own(buf, ss, rs):
+        for bit in bits:
+            dp_send(buf, ss, rs, 0, bit).start()
+
+    def dp_rest(buf, ss, rs):
+        here = set()
+        for bit in bits:
+            for off in range(2 * bit, m, 2 * bit):
+                if off not in here:
+                    dp_arrived(buf, ss, rs, off)
+                    here.add(off)
+                dp_send(buf, ss, rs, off, bit).start()
+        for off in range(1, m):
+            if off not in here:
+                dp_arrived(buf, ss, rs, off)
+
+    def dp_sent(buf, ss, rs):
+        for bit in bits:
+            for off in range(0, m, 2 * bit):
+                dp_send(buf, ss, rs, off, bit).wait_send()
 
     barrier = pltpu.get_barrier_semaphore()
 
@@ -141,6 +176,7 @@
     lax.fori_loop(1, n, greet_seq, 0)
     lax.fori_loop(1, m, greet_dp, 0)
 
+    loads[0].wait()
     dt = dt_ref[0]
     at_row = lax.broadcasted_iota(jnp.int32, (tokens, tokens), 0)
     at_col = lax.broadcasted_iota(jnp.int32, (tokens, tokens), 1)
@@ -159,7 +195,10 @@
     cum_col = joined([dot(low_mat, d, NT) for d in digits])
     dt_col = joined([dot(eye, d, NT) for d in digits])
     rate_row = arow_ref[...] * (1.0 / (8.0 * seq_len))
-    rate_col = acol_ref[...] * (1.0 / (8.0 * seq_len))
+    same = lax.broadcasted_iota(jnp.int32, (HEADS, HEADS), 0) == lax.broadcasted_iota(
+        jnp.int32, (HEADS, HEADS), 1
+    )
+    rate_col = jnp.sum(jnp.where(same, rate_row, 0.0), axis=1, keepdims=True)
     weight = jnp.sqrt(one_minus_exp(2.0 * (rate_row * dt_col.astype(f32))))
     head = jnp.exp(-(rate_row * cum_col.astype(f32)))
     tail = jnp.exp(-(rate_row * (cum_col[tokens - 1 :, :] - cum_col).astype(f32)))
@@ -168,6 +207,8 @@
     )
     weight_w, head_w, tail_w = widen(weight), widen(head), widen(tail)
 
+    for load in loads[1:4]:
+        load.wait()
     b = b_ref[0]
     c = c_ref[0]
     weighted = x_ref[0].astype(f32) * weight_w
@@ -180,6 +221,7 @@
     pl.semaphore_wait(barrier, n - 1 + m - 1)
     seq_start(fsend, frecv, f_ss, f_rs)
 
+    loads[4].wait()
     grad = g_ref[0]
     for d in range(m):
         gsend[d] = grad[:, d * cols : (d + 1) * cols].astype(f32)
@@ -195,6 +237,7 @@
     lax.fori_loop(1, m, g_start, 0)
     gall[dp] = gsend[dp]
 
+    loads[5].wait()
     grad_y = dot(grad, w_ref[...], NT).astype(bf16)
     grad_dec = (grad_y.astype(f32) * head_w).astype(bf16)
     own_adj = dot(grad_dec, c, TN)
@@ -245,30 +288,110 @@
     seq_wait(fback, fin, fb_ss, fb_rs)
     state_in = fin[...].reshape(CHANNELS, STATE).astype(bf16)
     out = (y_intra + dot(c, state_in, NT) * head_w).astype(bf16)
+    for j in ORDER:
+        oall[j, dp] = out[:, j * STATE : (j + 1) * STATE].astype(f32)
+        dp_own(oall.at[j], o_ss.at[j], o_rs.at[j])
     out_ref[0] = out
-    oall[dp] = out.astype(f32)
-    dp_gather(oall, o_ss, o_rs)
+    stores[0].start()
     lax.fori_loop(1, m, g_wait, 0)
-    total = jnp.zeros((CHANNELS, cols), f32)
-    for d in range(m):
-        total = total + dot(oall[d].astype(bf16), gall[d].astype(bf16), TN)
-    part[...] = total.reshape(n, rows, cols)
-    seq_start(part, rsbuf, r_ss, r_rs)
+
+    def to_partner(p, wait):
+        return pltpu.make_async_remote_copy(
+            src_ref=part.at[2 * p + 1 - y],
+            dst_ref=ybuf.at[p],
+            send_sem=y_ss.at[p],
+            recv_sem=y_rs.at[p],
+            device_id={"seq": 2 * z + 1 - y},
+            device_id_type=MESH,
+        )
+
+    def to_owner(p, source):
+        return pltpu.make_async_remote_copy(
+            src_ref=part.at[2 * p + y],
+            dst_ref=rsbuf.at[source],
+            send_sem=r_ss.at[p],
+            recv_sem=r_rs.at[source],
+            device_id={"seq": 2 * p + y},
+            device_id_type=MESH,
+        )
+
+    per = pairs // CHUNKS
+
+    def multiply(j):
+        dp_rest(oall.at[j], o_ss.at[j], o_rs.at[j])
+        total = jnp.zeros((STATE, cols), f32)
+        for d in range(m):
+            total = total + dot(oall[j, d].astype(bf16), gall[d].astype(bf16), TN)
+        part[2 * per * j : 2 * per * (j + 1)] = total.reshape(2 * per, rows, cols)
+
+        def body(p, carry):
+            to_partner(p, False).start()
+            return carry
+
+        lax.fori_loop(per * j, per * (j + 1), body, 0)
+
+    def join(j):
+        def body(p, carry):
+            to_partner(p, True).wait_recv()
+            part[2 * p + y] = part[2 * p + y] + ybuf[p]
+
+            @pl.when(p != z)
+            def _():
+                to_owner(p, z).start()
+
+            return carry
+
+        lax.fori_loop(per * j, per * (j + 1), body, 0)
+
+    for at, j in enumerate(ORDER):
+        multiply(j)
+        if at:
+            join(ORDER[at - 1])
+    join(ORDER[-1])
 
     gread_ref[0] = (read_intra + dot(grad_dec, state_in)).astype(bf16)
+    stores[3].start()
     seq_wait(aback, ain, ab_ss, ab_rs)
     adj_in = ain[...].reshape(CHANNELS, STATE).astype(bf16)
     gwrite_ref[0] = (write_intra + dot(tailed, adj_in)).astype(bf16)
+    stores[2].start()
     gin_ref[0] = ((gx_intra + tail_w * dot(b, adj_in, NT)) * weight_w).astype(bf16)
+    stores[1].start()
 
     def add_rows(k, acc):
-        seq_copy(part, rsbuf, r_ss, r_rs, k, True).wait()
-        return acc + rsbuf[lax.rem(me + n - k, n)]
-
-    gwall[dp] = lax.fori_loop(1, n, add_rows, part[me])
-    dp_gather(gwall, w_ss, w_rs)
+        source = lax.rem(z + k, pairs)
+        to_owner(source, source).wait()
+        return acc + rsbuf[source]
+
+    gwall[dp] = lax.fori_loop(1, pairs, add_rows, part[me])
+    dp_own(gwall, w_ss, w_rs)
+    dp_rest(gwall, w_ss, w_rs)
     for d in range(m):
         gw_ref[:, d * cols : (d + 1) * cols] = gwall[d]
+    stores[4].start()
+
+    def sent(p, carry):
+        to_partner(p, True).wait_send()
+        return carry
+
+    lax.fori_loop(0, pairs, sent, 0)
+    for j in ORDER:
+        dp_sent(oall.at[j], o_ss.at[j], o_rs.at[j])
+    dp_sent(gwall, w_ss, w_rs)
+    for store in stores:
+        store.wait()
+
+
+def settle(*refs):
+    count = len(refs) // 2
+    sem = refs[-1]
+    copies = [
+        pltpu.make_async_copy(refs[i], refs[count + i], sem.at[i]) for i in range(count)
+    ]
+    for copy in copies:
+        copy.start()
+    for copy in copies:
+        copy.wait()
 
 
 def solution(mesh):
@@ -277,23 +400,28 @@
     def shards(inputs, write_vecs, read_vecs, dt_code, a_rate, w_out, grad_out):
         tokens, width = inputs.shape[1], grad_out.shape[2]
         rows, cols = CHANNELS // n, width // m
+        hbm = pl.BlockSpec(memory_space=pltpu.MemorySpace.HBM)
         vm = pl.BlockSpec(memory_space=pltpu.VMEM)
         sems = []
-        for count in (m, n, n, n, n, m, n, m):
-            sems += [pltpu.SemaphoreType.DMA((count,))] * 2
+        for shape in ((m,), (n,), (n,), (n,), (n,), (CHUNKS, m), (n // 2,), (n // 2,), (m,)):
+            sems += [pltpu.SemaphoreType.DMA(shape)] * 2
         wide, plain = (n, rows + HEADS, STATE), (n, rows, STATE)
-        return pl.pallas_call(
+        results = (
+            jax.ShapeDtypeStruct((1, tokens, CHANNELS), bf16),
+            jax.ShapeDtypeStruct((1, tokens, CHANNELS), bf16),
+            jax.ShapeDtypeStruct((1, tokens, STATE), bf16),
+            jax.ShapeDtypeStruct((1, tokens, STATE), bf16),
+            jax.ShapeDtypeStruct((rows, width), f32),
+        )
+        args = (inputs, write_vecs, read_vecs, dt_code, w_out, grad_out)
+        held = pl.pallas_call(
             functools.partial(kernel, n, m, float(tokens * n)),
-            out_shape=(
-                jax.ShapeDtypeStruct((1, tokens, CHANNELS), bf16),
-                jax.ShapeDtypeStruct((1, tokens, CHANNELS), bf16),
-                jax.ShapeDtypeStruct((1, tokens, STATE), bf16),
-                jax.ShapeDtypeStruct((1, tokens, STATE), bf16),
-                jax.ShapeDtypeStruct((rows, width), f32),
-            ),
-            in_specs=[vm] * 8,
-            out_specs=(vm,) * 5,
-            scratch_shapes=[
+            out_shape=results,
+            in_specs=[hbm] * 4 + [vm] + [hbm] * 2,
+            out_specs=(hbm,) * 5,
+            scratch_shapes=[pltpu.VMEM(a.shape, a.dtype) for a in args]
+            + [pltpu.VMEM(a.shape, a.dtype) for a in results]
+            + [
                 pltpu.VMEM((m, tokens, cols), f32),
                 pltpu.VMEM((m, tokens, cols), f32),
                 pltpu.VMEM(wide, f32),
@@ -304,26 +432,28 @@
                 pltpu.VMEM(wide, f32),
                 pltpu.VMEM(plain, f32),
                 pltpu.VMEM(plain, f32),
-                pltpu.VMEM((m, tokens, CHANNELS), f32),
+                pltpu.VMEM((CHUNKS, m, tokens, STATE), f32),
                 pltpu.VMEM((n, rows, cols), f32),
-                pltpu.VMEM((n, rows, cols), f32),
+                pltpu.VMEM((n // 2, rows, cols), f32),
+                pltpu.VMEM((n // 2, rows, cols), f32),
                 pltpu.VMEM((m, rows, cols), f32),
             ]
-            + sems,
+            + sems
+            + [pltpu.SemaphoreType.DMA((6,)), pltpu.SemaphoreType.DMA((5,))],
             compiler_params=pltpu.CompilerParams(
-                collective_id=0, has_side_effects=True, vmem_limit_bytes=48 * 1024 * 1024
+                collective_id=0, has_side_effects=True, vmem_limit_bytes=VMEM_BYTES
             ),
             name="scan_core",
-        )(
-            inputs,
-            write_vecs,
-            read_vecs,
-            dt_code,
-            a_rate.reshape(1, HEADS),
-            a_rate.reshape(HEADS, 1),
-            w_out,
-            grad_out,
-        )
+        )(inputs, write_vecs, read_vecs, dt_code, a_rate.reshape(1, HEADS), w_out, grad_out)
+        return pl.pallas_call(
+            settle,
+            out_shape=results,
+            in_specs=[hbm] * 5,
+            out_specs=(hbm,) * 5,
+            scratch_shapes=[pltpu.SemaphoreType.DMA((5,))],
+            compiler_params=pltpu.CompilerParams(vmem_limit_bytes=VMEM_BYTES),
+            name="settle",
+        )(*held)
 
     placed = (
         P("dp", "seq", None),

time: 98.3 us -> 113 us (1.15)
  Pallas kernels: 86 us -> 111 us
  local copies, waits for them, and re-layouts: 11.3 us -> 0 us
    pallas_call x0 -> x1, Pallas kernels: none -> 40.9 us  [shards(): pl.pallas_call(settle, out_shape=results, in_specs=[hbm] * 5, out_specs=(...]
    pallas_call x1, Pallas kernels: 86 us -> 70.1 us  [shards(): pl.pallas_call(functools.partial(kernel, n, m, float(tokens * n)), out_sh...]
    unnamed x19 -> x0, local copies, waits for them, and re-layouts: 10.5 us -> none
where the time goes in v2:
time: 113 us; the launch traced here: 112 us
  Pallas kernels  111 us (98%)
    pallas_call x1, Pallas kernels, shards(): pl.pallas_call(functools.partial(kernel, n, m, float(tokens * n)), out_sh...  70.1 us
    pallas_call x1, Pallas kernels, shards(): pl.pallas_call(settle, out_shape=results, in_specs=[hbm] * 5, out_specs=(...  40.9 us

profile of v2, /device:TPU:13, one launch (start us, length us, event | category | flops | bytes accessed | tf_op | source)
XLA Modules:
  0.0 111.6 jit_solution(11896156760898488794)
XLA Ops:
  0.6 70.1 %scan_core.1 = (bf16[1,256,512]{2,1,0:T(8,128)(2,1)}, bf16[1,256,512]{2,1,0:T(8,128)(2,1)}, bf16[1,256,128]{2,1,0:T(8,128)(2,1)}, bf16[1,256,128]{2,1,0:T(8,128)(2,1)}, f32[64,2560]{1,0:T(8,128)}) custom-call(bf16[1,256,512]{2,1,0:T(8,128)(2,1)} %x_hbm.1, bf16[1,256,128]{2,1,0:T(8,128)(2,1)} %b_hbm.1, bf16[1,256,128]{2,1,0:T(8,128)(2,1)} %c_hbm.1, ...), custom_call_target="tpu_custom_call" | custom-call | tf_op jit(solution)/shard_map/scan_core/pallas_call | solution.py:417
  70.7 40.9 %settle.1 = (bf16[1,256,512]{2,1,0:T(8,128)(2,1)}, bf16[1,256,512]{2,1,0:T(8,128)(2,1)}, bf16[1,256,128]{2,1,0:T(8,128)(2,1)}, bf16[1,256,128]{2,1,0:T(8,128)(2,1)}, f32[64,2560]{1,0:T(8,128)}) custom-call(bf16[1,256,512]{2,1,0:T(8,128)(2,1)} %get-tuple-element.10.refs_0_, bf16[1,256,512]{2,1,0:T(8,128)(2,1)} %get-tuple-element.11.refs_1_, ...), custom_call_target="tpu_custom_call" | custom-call | tf_op jit(solution)/shard_map/settle/pallas_call | solution.py:448
